TPU v7x, 256 devices: a whole 4x4x8 slice. The times are simulated.
256 devices in a mesh: az: 128 (over z, x, y_hi, core), dep: 2 (over y_lo).
Axes of the slice: x: 4, y: 4 (y_hi: 2, y_lo: 2; y = y_hi * 2 + y_lo), z: 8, core: 2. Of those that a mesh axis runs over, the one named last changes fastest.
Arguments:
- field: float32 [8192, 2, 1024], P('az', None, 'dep'), may hold values from -6 to 6
- brick_speed: bfloat16 [32768, 1024], P('az', 'dep'), may hold values from -40 to 40
- send_index: int32 [128, 128, 32], P('az'), may hold values from 0 to 255
- send_count: int32 [128, 128], P('az'), may hold values from 0 to 32, as said below
- weights: bfloat16 [8192, 4, 4096], P('az'), may hold values from 0 to 1, as said below
- propagator: bfloat16 [2, 2, 1024, 1024], replicated, may hold values from -1 to 1
Outputs:
- pressure: float32 [8192, 2, 1024], P('az', None, 'dep')
Inputs may be any that keep to these rules, and one draw needn't show every extreme that they name: `send_count`: 32 or fewer columns from one brick to one sector; one sector receives 32 from every brick. Nonnegative interpolation weights.
All inputs are finite; a program needn't handle non-finite values.
Results may differ from a plain program's by a relative error of at most 0.025.
Values may be sent and summed in bfloat16 or wider, within the bound.
No kernel may reach another device: no remote copies, remote signals or barrier semaphores. Data moves between devices by JAX's collectives and lax.ppermute only.
A program may use at most 64 MiB of HBM per device.

v0:
```python
import jax
import jax.numpy as jnp
from jax import lax
from jax.sharding import PartitionSpec as P

angle_rate = 200.0 / 1500.0
couple_real = 0.1
couple_imag = 0.15


def padded_2(cells, sides, width):
    for axis, dim in sides:
        count = lax.axis_size(axis)
        head = lax.slice_in_dim(cells, 0, width, axis=dim)
        tail = lax.slice_in_dim(cells, cells.shape[dim] - width, cells.shape[dim], axis=dim)
        cells = jnp.concatenate(
            [
                lax.ppermute(tail, axis, [(i, (i + 1) % count) for i in range(count)]),
                cells,
                lax.ppermute(head, axis, [((i + 1) % count, i) for i in range(count)]),
            ],
            axis=dim,
        )
    return cells


def apply_screen(field, angle):
    cosine = jnp.cos(angle)
    sine = jnp.sin(angle)
    real_part = field[:, 0] * cosine - field[:, 1] * sine
    imag_part = field[:, 0] * sine + field[:, 1] * cosine
    return jnp.stack([real_part, imag_part], axis=1)


def azimuth_couple(padded, rows):
    laplace = (
        -padded[0:rows]
        + 16.0 * padded[1 : rows + 1]
        - 30.0 * padded[2 : rows + 2]
        + 16.0 * padded[3 : rows + 3]
        - padded[4 : rows + 4]
    ) / 12.0
    centre = padded[2 : rows + 2]
    real_part = centre[:, 0] + couple_real * laplace[:, 0] - couple_imag * laplace[:, 1]
    imag_part = centre[:, 1] + couple_real * laplace[:, 1] + couple_imag * laplace[:, 0]
    return jnp.stack([real_part, imag_part], axis=1)


def combine_parts(mixed):
    real_part = mixed[:, 0, 0] - mixed[:, 1, 1]
    imag_part = mixed[:, 0, 1] + mixed[:, 1, 0]
    return jnp.stack([real_part, imag_part], axis=1)


def propagate_block(field, columns):
    rounded = field.astype(jnp.bfloat16)
    mixed = jnp.einsum(
        "acz,pzw->acpw",
        lax.all_gather(rounded, "dep", axis=2, tiled=True),
        columns,
        preferred_element_type=jnp.float32,
    )
    return combine_parts(mixed)


def per_device(field, brick_speed, send_index, send_count, weights, propagator):
    depth_block = brick_speed.shape[1]
    chosen = send_index[0]
    limit = send_count[0]
    packed = brick_speed[chosen]
    slots = lax.broadcasted_iota(jnp.int32, chosen.shape, 1)
    keep = (slots < limit[:, None])[:, :, None]
    packed = jnp.where(keep, packed, jnp.zeros_like(packed))
    piece = lax.all_to_all(packed, "az", split_axis=0, concat_axis=0, tiled=True)
    flat = piece.reshape(piece.shape[0] * piece.shape[1], piece.shape[2])
    speed = jnp.einsum("akm,mz->akz", weights, flat, preferred_element_type=jnp.float32)
    angle = -angle_rate * speed
    factors = propagator.shape[0]
    steps = angle.shape[1]
    out_start = lax.axis_index("dep") * depth_block
    column_blocks = [
        lax.dynamic_slice_in_dim(propagator[factor], out_start, depth_block, 2)
        for factor in range(factors)
    ]
    rows = field.shape[0]
    for step in range(steps):
        field = apply_screen(field, angle[:, step, :])
        padded = padded_2(field.astype(jnp.bfloat16), (("az", 0),), 2).astype(field.dtype)
        field = azimuth_couple(padded, rows)
        for factor in range(factors):
            field = propagate_block(field, column_blocks[factor])
    return field


def solution(mesh):
    placed = (
        P("az", None, "dep"),
        P("az", "dep"),
        P("az", None, None),
        P("az", None),
        P("az", None, None),
        P(),
    )
    return jax.shard_map(
        per_device, mesh=mesh, in_specs=placed, out_specs=P("az", None, "dep"), check_vma=False
    )
```

profile of v0, /device:TPU:8, one launch (start us, length us, event | category | flops | bytes accessed | tf_op | source)
XLA Modules:
  0.0 237.7 jit_solution(14931970678833933907)
XLA Ops:
  0.0 0.9 compare_select_fusion
  0.9 0.7 iota_compare_fusion
  1.6 0.1 copy.12
  1.7 0.1 reshape.366
  1.8 18.5 %gather_fusion = bf16[4096,512]{1,0:T(8,128)(2,1)} fusion(bf16[256,512]{1,0:T(8,128)(2,1)} %param.7, s32[4096]{0:T(1024)S(1)} %broadcast_clamp_fusion), kind=kCustom, calls=%fused_computation | custom fusion | bytes 8404992 | tf_op jit(solution)/shard_map/gather | solution.py:70
  20.3 3.9 %broadcast_select_fusion = bf16[128,32,512]{2,1,0:T(8,128)(2,1)} fusion(bf16[128,32,512]{2,1,0:T(8,128)(2,1)} %bitcast.128, pred[128,32]{1,0:T(8,128)(4,1)S(1)} %iota_compare_fusion), kind=kLoop, calls=%fused_computation.1 | loop fusion | flops 2097152 | bytes 8392704 | tf_op jit(solution)/shard_map/jit(_where)/select_n | solution.py:73
  24.2 15.6 %all-to-all-start = ((bf16[128,32,512]{2,1,0:T(8,128)(2,1)}), bf16[128,32,512]{2,1,0:T(8,128)(2,1)}, u32[]{:S(2)}, u32[]{:S(2)}) async-start(bf16[128,32,512]{2,1,0:T(8,128)(2,1)} %broadcast_select_fusion), calls=%async_computation | async-start | bytes 8388608 | tf_op jit(solution)/shard_map/all_to_all | solution.py:74
  39.8 0.2 fusion.105
  40.0 97.1 %all-to-all-done = bf16[128,32,512]{2,1,0:T(8,128)(2,1)} async-done(((bf16[128,32,512]{2,1,0:T(8,128)(2,1)}), bf16[128,32,512]{2,1,0:T(8,128)(2,1)}, u32[]{:S(2)}, u32[]{:S(2)}) %all-to-all-start) | async-done | bytes 4194336 | tf_op jit(solution)/shard_map/all_to_all | solution.py:74
  137.1 3.7 %fusion.29 = f32[64,4,512]{2,0,1:T(8,128)S(1)} fusion(bf16[4096,512,1]{1,0,2:T(8,128)(2,1)} %bitcast.4, bf16[64,4,4096]{2,1,0:T(4,128)(2,1)S(1)} %copy-done), kind=kOutput, calls=%fused_computation.29 | convolution fusion | flops 1073872896 | bytes 6815744 | tf_op jit(solution)/shard_map/akm,mz->akz/dot_general | solution.py:76
  140.8 0.5 subtract_convert_fusion.3
  141.3 0.1 collective-permute-start
  141.4 7.5 %collective-permute-start.1 = (bf16[2,2,512]{2,0,1:T(2,128)(2,1)S(1)}, bf16[2,2,512]{2,0,1:T(2,128)(2,1)S(1)}, u32[]{:S(2)}, u32[]{:S(2)}) collective-permute-start(bf16[2,2,512]{2,0,1:T(2,128)(2,1)S(1)} %get-tuple-element.42), channel_id=1, source_target_pairs={{2,0},{4,2},{6,4},{8,6},{10,8},{12,10},{14,12},{16,14},{18,16},{20... | collective-permute-start | bytes 12296 | tf_op jit(solution)/shard_map/ppermute | solution.py:20
  148.9 6.0 %fusion.104 = (bf16[1,2,1024,1024]{3,2,1,0:T(8,128)(2,1)}, bf16[1,2,1024,1024]{3,2,1,0:T(8,128)(2,1)}) fusion(bf16[2,2,1024,1024]{3,2,1,0:T(8,128)(2,1)} %param.11), kind=kLoop, calls=%fused_computation.186 | loop fusion | bytes 16777216 | tf_op jit(solution)/shard_map/slice | solution.py:82
  154.9 0.2 fusion.44
  155.1 7.0 %all_gather.24 = bf16[64,2,1024]{2,0,1:T(8,128)(2,1)S(1)} all-gather(bf16[64,2,512]{2,0,1:T(8,128)(2,1)S(1)} %pad_maximum_fusion.1), channel_id=1, replica_groups=mesh['az'=128,'dep'=2] {'dep'}, dimensions={2}, use_global_device_ids=true | all-gather | bytes 393216 | tf_op jit(solution)/shard_map/all_gather | solution.py:59
  162.1 2.0 fusion.14
  164.3 5.8 %all_gather.25 = bf16[64,2,1024]{2,0,1:T(8,128)(2,1)S(1)} all-gather(bf16[64,2,512]{2,0,1:T(8,128)(2,1)S(1)} %pad_maximum_fusion.2), channel_id=1, replica_groups=mesh['az'=128,'dep'=2] {'dep'}, dimensions={2}, use_global_device_ids=true | all-gather | bytes 393216 | tf_op jit(solution)/shard_map/all_gather | solution.py:59
  170.1 0.5 fusion.6
  170.5 0.5 subtract_convert_fusion.2
  171.1 0.1 collective-permute-start.2
  171.2 7.5 %collective-permute-start.3 = (bf16[2,2,512]{2,0,1:T(2,128)(2,1)S(1)}, bf16[2,2,512]{2,0,1:T(2,128)(2,1)S(1)}, u32[]{:S(2)}, u32[]{:S(2)}) collective-permute-start(bf16[2,2,512]{2,0,1:T(2,128)(2,1)S(1)} %get-tuple-element.40), channel_id=1, source_target_pairs={{2,0},{4,2},{6,4},{8,6},{10,8},{12,10},{14,12},{16,14},{18,16},{20... | collective-permute-start | bytes 12296 | tf_op jit(solution)/shard_map/ppermute | solution.py:20
  178.6 1.3 collective-permute-done.2
  180.0 0.2 fusion.40
  180.1 0.1 fusion.79
  180.2 5.6 %all_gather.26 = bf16[64,2,1024]{2,0,1:T(8,128)(2,1)S(1)} all-gather(bf16[64,2,512]{2,0,1:T(8,128)(2,1)S(1)} %pad_maximum_fusion.3), channel_id=1, replica_groups=mesh['az'=128,'dep'=2] {'dep'}, dimensions={2}, use_global_device_ids=true | all-gather | bytes 393216 | tf_op jit(solution)/shard_map/all_gather | solution.py:59
  185.9 0.5 fusion.12
  186.4 5.8 %all_gather.27 = bf16[64,2,1024]{2,0,1:T(8,128)(2,1)S(1)} all-gather(bf16[64,2,512]{2,0,1:T(8,128)(2,1)S(1)} %pad_maximum_fusion.4), channel_id=1, replica_groups=mesh['az'=128,'dep'=2] {'dep'}, dimensions={2}, use_global_device_ids=true | all-gather | bytes 393216 | tf_op jit(solution)/shard_map/all_gather | solution.py:59
  192.2 0.5 fusion.4
  192.7 0.5 subtract_convert_fusion.1
  193.2 0.1 collective-permute-start.4
  193.3 7.5 %collective-permute-start.5 = (bf16[2,2,512]{2,0,1:T(2,128)(2,1)S(1)}, bf16[2,2,512]{2,0,1:T(2,128)(2,1)S(1)}, u32[]{:S(2)}, u32[]{:S(2)}) collective-permute-start(bf16[2,2,512]{2,0,1:T(2,128)(2,1)S(1)} %get-tuple-element.38), channel_id=1, source_target_pairs={{2,0},{4,2},{6,4},{8,6},{10,8},{12,10},{14,12},{16,14},{18,16},{20... | collective-permute-start | bytes 12296 | tf_op jit(solution)/shard_map/ppermute | solution.py:20
  200.8 1.3 collective-permute-done.4
  202.2 0.2 fusion.36
  202.4 5.6 %all_gather.28 = bf16[64,2,1024]{2,0,1:T(8,128)(2,1)S(1)} all-gather(bf16[64,2,512]{2,0,1:T(8,128)(2,1)S(1)} %pad_maximum_fusion.5), channel_id=1, replica_groups=mesh['az'=128,'dep'=2] {'dep'}, dimensions={2}, use_global_device_ids=true | all-gather | bytes 393216 | tf_op jit(solution)/shard_map/all_gather | solution.py:59
  208.1 0.5 fusion.10
  208.6 5.6 %all_gather.29 = bf16[64,2,1024]{2,0,1:T(8,128)(2,1)S(1)} all-gather(bf16[64,2,512]{2,0,1:T(8,128)(2,1)S(1)} %pad_maximum_fusion.6), channel_id=1, replica_groups=mesh['az'=128,'dep'=2] {'dep'}, dimensions={2}, use_global_device_ids=true | all-gather | bytes 393216 | tf_op jit(solution)/shard_map/all_gather | solution.py:59
  214.2 0.5 fusion.2
  214.7 0.5 subtract_convert_fusion
  215.2 0.1 collective-permute-start.6
  215.3 7.5 %collective-permute-start.7 = (bf16[2,2,512]{2,0,1:T(2,128)(2,1)S(1)}, bf16[2,2,512]{2,0,1:T(2,128)(2,1)S(1)}, u32[]{:S(2)}, u32[]{:S(2)}) collective-permute-start(bf16[2,2,512]{2,0,1:T(2,128)(2,1)S(1)} %get-tuple-element.36), channel_id=1, source_target_pairs={{2,0},{4,2},{6,4},{8,6},{10,8},{12,10},{14,12},{16,14},{18,16},{20... | collective-permute-start | bytes 12296 | tf_op jit(solution)/shard_map/ppermute | solution.py:20
  222.8 1.3 collective-permute-done.6
  224.2 0.2 fusion.32
  224.4 5.6 %all_gather.30 = bf16[64,2,1024]{2,0,1:T(8,128)(2,1)S(1)} all-gather(bf16[64,2,512]{2,0,1:T(8,128)(2,1)S(1)} %pad_maximum_fusion.7), channel_id=1, replica_groups=mesh['az'=128,'dep'=2] {'dep'}, dimensions={2}, use_global_device_ids=true | all-gather | bytes 393216 | tf_op jit(solution)/shard_map/all_gather | solution.py:59
  230.0 0.5 fusion.8
  230.6 5.6 %all_gather.31 = bf16[64,2,1024]{2,0,1:T(8,128)(2,1)S(1)} all-gather(bf16[64,2,512]{2,0,1:T(8,128)(2,1)S(1)} %pad_maximum_fusion.8), channel_id=1, replica_groups=mesh['az'=128,'dep'=2] {'dep'}, dimensions={2}, use_global_device_ids=true | all-gather | bytes 393216 | tf_op jit(solution)/shard_map/all_gather | solution.py:59
  236.2 0.5 fusion
  236.8 0.9 copy.15
  (39 shorter events, 0.9 us)
Async XLA Ops:
  0.0 137.1 %copy-start = (bf16[64,4,4096]{2,1,0:T(4,128)(2,1)S(1)}, bf16[64,4,4096]{2,1,0:T(4,128)(2,1)}, u32[]{:S(2)}) copy-start(bf16[64,4,4096]{2,1,0:T(4,128)(2,1)} %param.10) | copy-start | bytes 6291460
  24.2 15.6 %copy-start.3 = (f32[64,2,512]{2,1,0:T(2,128)S(1)}, f32[64,2,512]{2,1,0:T(2,128)}, u32[]{:S(2)}) copy-start(f32[64,2,512]{2,1,0:T(2,128)} %param.6) | copy-start | bytes 786436
  24.2 112.9 %all-to-all-start = ((bf16[128,32,512]{2,1,0:T(8,128)(2,1)}), bf16[128,32,512]{2,1,0:T(8,128)(2,1)}, u32[]{:S(2)}, u32[]{:S(2)}) async-start(bf16[128,32,512]{2,1,0:T(8,128)(2,1)} %broadcast_select_fusion), calls=%async_computation | async-start | bytes 8388608 | tf_op jit(solution)/shard_map/all_to_all | solution.py:74
  141.3 13.5 %collective-permute-start = (bf16[2,2,512]{2,0,1:T(2,128)(2,1)S(1)}, bf16[2,2,512]{2,0,1:T(2,128)(2,1)S(1)}, u32[]{:S(2)}, u32[]{:S(2)}) collective-permute-start(bf16[2,2,512]{2,0,1:T(2,128)(2,1)S(1)} %get-tuple-element.41), channel_id=1, source_target_pairs={{0,2},{2,4},{4,6},{6,8},{8,10},{10,12},{12,14},{14,16},{16,18},{18... | collective-permute-start | bytes 12296 | tf_op jit(solution)/shard_map/ppermute | solution.py:18
  141.4 13.4 %collective-permute-start.1 = (bf16[2,2,512]{2,0,1:T(2,128)(2,1)S(1)}, bf16[2,2,512]{2,0,1:T(2,128)(2,1)S(1)}, u32[]{:S(2)}, u32[]{:S(2)}) collective-permute-start(bf16[2,2,512]{2,0,1:T(2,128)(2,1)S(1)} %get-tuple-element.42), channel_id=1, source_target_pairs={{2,0},{4,2},{6,4},{8,6},{10,8},{12,10},{14,12},{16,14},{18,16},{20... | collective-permute-start | bytes 12296 | tf_op jit(solution)/shard_map/ppermute | solution.py:20
  154.8 15.3 %copy-start.1 = (bf16[1,2,1024,1024]{3,2,1,0:T(8,128)(2,1)S(1)}, bf16[1,2,1024,1024]{3,2,1,0:T(8,128)(2,1)}, u32[]{:S(2)}) copy-start(bf16[1,2,1024,1024]{3,2,1,0:T(8,128)(2,1)} %get-tuple-element.6) | copy-start | bytes 12582916
  164.2 21.7 %copy-start.2 = (bf16[1,2,1024,1024]{3,2,1,0:T(8,128)(2,1)S(1)}, bf16[1,2,1024,1024]{3,2,1,0:T(8,128)(2,1)}, u32[]{:S(2)}) copy-start(bf16[1,2,1024,1024]{3,2,1,0:T(8,128)(2,1)} %get-tuple-element.5) | copy-start | bytes 12582916
  171.1 8.8 %collective-permute-start.2 = (bf16[2,2,512]{2,0,1:T(2,128)(2,1)S(1)}, bf16[2,2,512]{2,0,1:T(2,128)(2,1)S(1)}, u32[]{:S(2)}, u32[]{:S(2)}) collective-permute-start(bf16[2,2,512]{2,0,1:T(2,128)(2,1)S(1)} %get-tuple-element.39), channel_id=1, source_target_pairs={{0,2},{2,4},{4,6},{6,8},{8,10},{10,12},{12,14},{14,16},{16,18},{18... | collective-permute-start | bytes 12296 | tf_op jit(solution)/shard_map/ppermute | solution.py:18
  171.2 8.8 %collective-permute-start.3 = (bf16[2,2,512]{2,0,1:T(2,128)(2,1)S(1)}, bf16[2,2,512]{2,0,1:T(2,128)(2,1)S(1)}, u32[]{:S(2)}, u32[]{:S(2)}) collective-permute-start(bf16[2,2,512]{2,0,1:T(2,128)(2,1)S(1)} %get-tuple-element.40), channel_id=1, source_target_pairs={{2,0},{4,2},{6,4},{8,6},{10,8},{12,10},{14,12},{16,14},{18,16},{20... | collective-permute-start | bytes 12296 | tf_op jit(solution)/shard_map/ppermute | solution.py:20
  193.2 8.8 %collective-permute-start.4 = (bf16[2,2,512]{2,0,1:T(2,128)(2,1)S(1)}, bf16[2,2,512]{2,0,1:T(2,128)(2,1)S(1)}, u32[]{:S(2)}, u32[]{:S(2)}) collective-permute-start(bf16[2,2,512]{2,0,1:T(2,128)(2,1)S(1)} %get-tuple-element.37), channel_id=1, source_target_pairs={{0,2},{2,4},{4,6},{6,8},{8,10},{10,12},{12,14},{14,16},{16,18},{18... | collective-permute-start | bytes 12296 | tf_op jit(solution)/shard_map/ppermute | solution.py:18
  193.3 8.8 %collective-permute-start.5 = (bf16[2,2,512]{2,0,1:T(2,128)(2,1)S(1)}, bf16[2,2,512]{2,0,1:T(2,128)(2,1)S(1)}, u32[]{:S(2)}, u32[]{:S(2)}) collective-permute-start(bf16[2,2,512]{2,0,1:T(2,128)(2,1)S(1)} %get-tuple-element.38), channel_id=1, source_target_pairs={{2,0},{4,2},{6,4},{8,6},{10,8},{12,10},{14,12},{16,14},{18,16},{20... | collective-permute-start | bytes 12296 | tf_op jit(solution)/shard_map/ppermute | solution.py:20
  215.2 8.8 %collective-permute-start.6 = (bf16[2,2,512]{2,0,1:T(2,128)(2,1)S(1)}, bf16[2,2,512]{2,0,1:T(2,128)(2,1)S(1)}, u32[]{:S(2)}, u32[]{:S(2)}) collective-permute-start(bf16[2,2,512]{2,0,1:T(2,128)(2,1)S(1)} %get-tuple-element.35), channel_id=1, source_target_pairs={{0,2},{2,4},{4,6},{6,8},{8,10},{10,12},{12,14},{14,16},{16,18},{18... | collective-permute-start | bytes 12296 | tf_op jit(solution)/shard_map/ppermute | solution.py:18
  215.3 8.8 %collective-permute-start.7 = (bf16[2,2,512]{2,0,1:T(2,128)(2,1)S(1)}, bf16[2,2,512]{2,0,1:T(2,128)(2,1)S(1)}, u32[]{:S(2)}, u32[]{:S(2)}) collective-permute-start(bf16[2,2,512]{2,0,1:T(2,128)(2,1)S(1)} %get-tuple-element.36), channel_id=1, source_target_pairs={{2,0},{4,2},{6,4},{8,6},{10,8},{12,10},{14,12},{16,14},{18,16},{20... | collective-permute-start | bytes 12296 | tf_op jit(solution)/shard_map/ppermute | solution.py:20
where the time goes:
time: 238 us
  waiting for transfers between devices  101 us (42%)
  blocking collectives  46.9 us (20%)
  starting transfers between devices  45.7 us (19%)
  local copies, waits for them, and re-layouts  25.8 us (11%)
  other arithmetic  8.91 us (4%)
  matrix products  8.91 us (4%)
    all_to_all x1, waiting for transfers between devices, per_device(): lax.all_to_all(packed, 'az', split_axis=0, concat_axis=0, tiled=True)  97.1 us
    all_gather x8, blocking collectives, propagate_block(): lax.all_gather(rounded, 'dep', axis=2, tiled=True)  46.9 us
    ppermute x4, starting transfers between devices, padded_2(): lax.ppermute(head, axis, [((i + 1) % count, i) for i in range(count)])  29.8 us
    gather x1, local copies, waits for them, and re-layouts, per_device(): packed = brick_speed[chosen]  18.5 us
    all_to_all x1, starting transfers between devices, per_device(): lax.all_to_all(packed, 'az', split_axis=0, concat_axis=0, tiled=True)  15.6 us
    slice x1, local copies, waits for them, and re-layouts, per_device(): propagator[factor]  5.95 us
    dot_general x8, matrix products, propagate_block(): jnp.einsum('acz,pzw->acpw', lax.all_gather(rounded, 'dep', axis=2, tiled=...  5.23 us
  transfers between devices with their start and end apart: 9, of which 4 were waited for; matrix products, arithmetic and copies ran while one was open for 3% of the time, Pallas kernels for 0%

commit v1 on v0

v1 whole, which is shorter than its diff:
```python
import math

import jax
import jax.numpy as jnp
from jax import lax
from jax.experimental import pallas as pl
from jax.experimental.pallas import tpu as pltpu
from jax.sharding import Mesh, PartitionSpec as P

angle_rate = 200.0 / 1500.0
couple_real = 0.1
couple_imag = 0.15

AXES = ("z", "x", "yh", "c", "yl")
SECTOR = ("z", "x", "yh", "c")
SIZES = (8, 4, 2, 2, 2)
HALO = 8
ROWS = 32
EXT = ROWS + 2 * HALO
NZ = 1024
STEPS = 4
FACTORS = 2
RING = 256


def encode_turns(speed):
    turns = speed * (-angle_rate / (2.0 * math.pi))
    code = jnp.round((turns - jnp.round(turns)) * 65536.0).astype(jnp.int32)
    return jnp.where(code > 32767, -32768, code).astype(jnp.int16)


def cos_sin(code):
    quadrant = (code + 8192) >> 14
    part = (code - (quadrant << 14)).astype(jnp.float32) * (1.0 / 16384.0)
    square = part * part
    h = math.pi / 2
    sine = part * (h + square * (-(h**3) / 6 + square * (h**5 / 120 - square * (h**7 / 5040))))
    cosine = 1.0 + square * (
        -(h**2) / 2 + square * (h**4 / 24 + square * (-(h**6) / 720 + square * (h**8 / 40320)))
    )
    odd = (quadrant & 1) == 1
    first = jnp.where(odd, sine, cosine)
    second = jnp.where(odd, cosine, sine)
    first = jnp.where(((quadrant + 1) & 2) == 2, -first, first)
    second = jnp.where((quadrant & 2) == 2, -second, second)
    return first, second


def march_kernel(
    side, code, code_left, code_right, field, field_left, field_right, factors, keep, send, state, padded, rounded
):
    state[:, 0:HALO] = field_left[...]
    state[:, HALO : HALO + ROWS] = field[...]
    state[:, HALO + ROWS : EXT] = field_right[...]
    padded[:, 0:HALO] = jnp.zeros((2, HALO, NZ), jnp.float32)
    padded[:, HALO + EXT :] = jnp.zeros((2, HALO, NZ), jnp.float32)
    pieces = ((code_left, HALO, 0), (code, ROWS, HALO), (code_right, HALO, HALO + ROWS))
    for step in range(STEPS):
        for ref, rows, start in pieces:
            value = ref[step * rows : (step + 1) * rows, :] if rows == ROWS else ref[...][step * rows : (step + 1) * rows, :]
            cosine, sine = cos_sin(value.astype(jnp.int32))
            real = state[0, start : start + rows]
            imag = state[1, start : start + rows]
            padded[0, HALO + start : HALO + start + rows] = real * cosine - imag * sine
            padded[1, HALO + start : HALO + start + rows] = real * sine + imag * cosine
        laplace = []
        for part in range(2):
            near = padded[part, HALO - 1 : HALO - 1 + EXT] + padded[part, HALO + 1 : HALO + 1 + EXT]
            far = padded[part, HALO - 2 : HALO - 2 + EXT] + padded[part, HALO + 2 : HALO + 2 + EXT]
            centre = padded[part, HALO : HALO + EXT]
            laplace.append((16.0 * near - far - 30.0 * centre) * (1.0 / 12.0))
        rounded[0:EXT] = (
            padded[0, HALO : HALO + EXT] + couple_real * laplace[0] - couple_imag * laplace[1]
        ).astype(jnp.bfloat16)
        rounded[EXT : 2 * EXT] = (
            padded[1, HALO : HALO + EXT] + couple_real * laplace[1] + couple_imag * laplace[0]
        ).astype(jnp.bfloat16)
        for factor in range(FACTORS):
            left = rounded[...]
            for column in range(0, NZ, 256):
                by_real = jnp.dot(
                    left, factors[factor, 0, :, column : column + 256], preferred_element_type=jnp.float32
                )
                by_imag = jnp.dot(
                    left, factors[factor, 1, :, column : column + 256], preferred_element_type=jnp.float32
                )
                state[0, :, column : column + 256] = by_real[:EXT] - by_imag[EXT:]
                state[1, :, column : column + 256] = by_imag[:EXT] + by_real[EXT:]
            if factor + 1 < FACTORS:
                rounded[0:EXT] = state[0].astype(jnp.bfloat16)
                rounded[EXT : 2 * EXT] = state[1].astype(jnp.bfloat16)
    low = state[:, HALO : HALO + ROWS, 0 : NZ // 2]
    high = state[:, HALO : HALO + ROWS, NZ // 2 :]
    first = side[0] == 0
    keep[...] = jnp.where(first, low, high)
    send[...] = jnp.where(first, high, low).astype(jnp.bfloat16)


def march(side, code, code_left, code_right, field, field_left, field_right, factors):
    half = (2, ROWS, NZ // 2)
    vmem = pl.BlockSpec(memory_space=pltpu.VMEM)
    return pl.pallas_call(
        march_kernel,
        out_shape=(jax.ShapeDtypeStruct(half, jnp.float32), jax.ShapeDtypeStruct(half, jnp.bfloat16)),
        in_specs=[pl.BlockSpec(memory_space=pltpu.SMEM)] + [vmem] * 7,
        out_specs=(vmem, vmem),
        scratch_shapes=[
            pltpu.VMEM((2, EXT, NZ), jnp.float32),
            pltpu.VMEM((2, EXT + 2 * HALO, NZ), jnp.float32),
            pltpu.VMEM((2 * EXT, NZ), jnp.bfloat16),
        ],
        compiler_params=pltpu.CompilerParams(vmem_limit_bytes=24 * 1024 * 1024),
        cost_estimate=pl.CostEstimate(
            flops=2 * 8 * 2 * EXT * NZ * 2 * NZ, bytes_accessed=10 * 1024 * 1024, transcendentals=0
        ),
        name="march",
    )(side, code, code_left, code_right, field, field_left, field_right, factors)


def swap_dep(value):
    return lax.ppermute(value, "yl", [(0, 1), (1, 0)])


def ring_step(value, shift):
    return lax.ppermute(value, AXES, [(i, (i + shift) % RING) for i in range(RING)])


def own_rows_all_depths(first, value, dim, depth_dim):
    top = lax.slice_in_dim(value, 0, ROWS, axis=dim)
    bottom = lax.slice_in_dim(value, ROWS, 2 * ROWS, axis=dim)
    mine = jnp.where(first, top, bottom)
    other = swap_dep(jnp.where(first, bottom, top))
    return jnp.where(
        first, jnp.concatenate([mine, other], depth_dim), jnp.concatenate([other, mine], depth_dim)
    )


def with_halo(value):
    before = ring_step(value[:, ROWS - HALO :], 1)
    after = ring_step(value[:, :HALO], -1)
    return before, after


def per_device(field, brick_speed, send_index, send_count, weights, propagator):
    first = lax.axis_index("yl") == 0
    chosen = send_index[0]
    limit = send_count[0]
    slots = lax.broadcasted_iota(jnp.int32, chosen.shape, 1)
    chosen = jnp.where(slots < limit[:, None], chosen, -1)
    columns = lax.broadcasted_iota(jnp.int32, chosen.shape + (brick_speed.shape[0],), 2)
    onehot = (chosen[:, :, None] == columns).astype(jnp.bfloat16)
    packed = jnp.einsum("dmc,cz->dmz", onehot, brick_speed, preferred_element_type=jnp.float32).astype(jnp.bfloat16)
    piece = lax.all_to_all(packed, SECTOR, split_axis=0, concat_axis=0, tiled=True)
    flat = piece.reshape(piece.shape[0] * piece.shape[1], piece.shape[2])

    own = own_rows_all_depths(first, field.transpose(1, 0, 2), 1, 2)
    own_left, own_right = with_halo(own)

    speed = jnp.einsum("akm,mz->kaz", weights, flat, preferred_element_type=jnp.float32)
    code = own_rows_all_depths(first, encode_turns(speed), 1, 2)
    code_left, code_right = with_halo(code)

    side = jnp.where(first, 0, 1).astype(jnp.int32).reshape(1)
    keep, send = march(
        side,
        code.reshape(STEPS * ROWS, NZ),
        code_left.reshape(STEPS * HALO, NZ),
        code_right.reshape(STEPS * HALO, NZ),
        own,
        own_left,
        own_right,
        propagator,
    )
    other = swap_dep(send).astype(jnp.float32)
    out = jnp.where(first, jnp.concatenate([keep, other], 1), jnp.concatenate([other, keep], 1))
    return out.transpose(1, 0, 2)


def solution(mesh):
    inner = Mesh(mesh.devices.reshape(SIZES), AXES)
    placed = (
        P(SECTOR, None, "yl"),
        P(SECTOR, "yl"),
        P(SECTOR, None, None),
        P(SECTOR, None),
        P(SECTOR, None, None),
        P(),
    )
    return jax.shard_map(
        per_device, mesh=inner, in_specs=placed, out_specs=P(SECTOR, None, "yl"), check_vma=False
    )
```

time: 238 us -> 158 us (0.66)
  blocking collectives: 46.9 us -> 0 us
  local copies, waits for them, and re-layouts: 25.8 us -> 8.75 us
  starting transfers between devices: 45.7 us -> 29.7 us
  other arithmetic: 8.91 us -> 1.16 us
  Pallas kernels: 0 us -> 7.37 us
  waiting for transfers between devices: 101 us -> 104 us
  matrix products: 8.91 us -> 6.22 us
    all_gather x8 -> x0, blocking collectives: 46.9 us -> none  [propagate_block(): lax.all_gather(rounded, 'dep', axis=2, tiled=True)]
    gather x1 -> x0, local copies, waits for them, and re-layouts: 18.5 us -> none  [per_device(): packed = brick_speed[chosen]]
    ppermute x8 -> x7, waiting for transfers between devices: 3.99 us -> 21.7 us  [the longest x3 17.6 us: swap_dep(): return lax.ppermute(value, 'yl', [(0, 1), (1, 0)])]
    ppermute x8 -> x7, starting transfers between devices: 30.2 us -> 14.2 us  [the longest x3 8.09 us: swap_dep(): return lax.ppermute(value, 'yl', [(0, 1), (1, 0)])]
    all_to_all x1, waiting for transfers between devices: 97.1 us -> 82.3 us  [per_device(): lax.all_to_all(packed, SECTOR, split_axis=0, concat_axis=0, tiled=True)]
    pallas_call x0 -> x1, Pallas kernels: none -> 7.37 us  [march(): pl.pallas_call(march_kernel, out_shape=(jax.ShapeDtypeStruct(half, jnp.fl...]
    slice x2, local copies, waits for them, and re-layouts: 6.16 us -> 0.02 us  [with_halo(): after = ring_step(value[:, :HALO], -1)]
    convert_element_type x0 -> x1, local copies, waits for them, and re-layouts: none -> 4.38 us  [per_device(): jnp.einsum('dmc,cz->dmz', onehot, brick_speed, preferred_element_type=jnp...]
  transfers between devices with their start and end apart: 9 -> 8, of which waited for: 4 -> 6; matrix products, arithmetic and copies ran while one was open for 3% -> 0% of each run, Pallas kernels for 0% -> 0%
where the time goes in v1:
time: 158 us; the launch traced here: 157 us
  waiting for transfers between devices  104 us (66%)
  starting transfers between devices  29.7 us (19%)
  local copies, waits for them, and re-layouts  8.75 us (6%)
  Pallas kernels  7.37 us (5%)
  matrix products  6.22 us (4%)
    all_to_all x1, waiting for transfers between devices, per_device(): lax.all_to_all(packed, SECTOR, split_axis=0, concat_axis=0, tiled=True)  82.3 us
    ppermute x3, waiting for transfers between devices, swap_dep(): return lax.ppermute(value, 'yl', [(0, 1), (1, 0)])  17.6 us
    all_to_all x1, starting transfers between devices, per_device(): lax.all_to_all(packed, SECTOR, split_axis=0, concat_axis=0, tiled=True)  15.6 us
    ppermute x3, starting transfers between devices, swap_dep(): return lax.ppermute(value, 'yl', [(0, 1), (1, 0)])  8.09 us
    pallas_call x1, Pallas kernels, march(): pl.pallas_call(march_kernel, out_shape=(jax.ShapeDtypeStruct(half, jnp.fl...  7.37 us
    ppermute x4, starting transfers between devices, ring_step(): lax.ppermute(value, AXES, [(i, (i + shift) % RING) for i in range(RING)])  6.1 us
    convert_element_type x1, local copies, waits for them, and re-layouts, per_device(): jnp.einsum('dmc,cz->dmz', onehot, brick_speed, preferred_element_type=jnp...  4.38 us
    ppermute x4, waiting for transfers between devices, ring_step(): lax.ppermute(value, AXES, [(i, (i + shift) % RING) for i in range(RING)])  4.15 us
  transfers between devices with their start and end apart: 8, of which 6 were waited for; matrix products, arithmetic and copies ran while one was open for 0% of the time, Pallas kernels for 0%

profile of v1, /device:TPU:8, one launch (start us, length us, event | category | flops | bytes accessed | tf_op | source)
XLA Modules:
  0.0 157.4 jit_solution(12409431188268204388)
XLA Ops:
  0.0 0.0 copy-start
  0.0 0.9 bitcast_select_fusion
  0.9 2.5 %fusion.1 = bf16[128,32,512]{2,0,1:T(8,128)(2,1)S(1)} fusion(s32[128,32]{0,1:T(8,128)S(1)} %bitcast_select_fusion, bf16[256,512]{1,0:T(8,128)(2,1)} %param.7), kind=kOutput, calls=%fused_computation.2 | convolution fusion | flops 1076887552 | bytes 4472832 | tf_op jit(solution)/shard_map/dmc,cz->dmz/dot_general | solution.py:152
  3.4 4.4 %copy.14 = bf16[128,32,512]{2,1,0:T(8,128)(2,1)} copy(bf16[128,32,512]{2,0,1:T(8,128)(2,1)S(1)} %fusion.1) | data formatting | bytes 8388608 | tf_op jit(solution)/shard_map/convert_element_type | solution.py:152
  7.7 0.0 copy-start.2
  7.7 15.6 %all-to-all-start = ((bf16[128,32,512]{2,1,0:T(8,128)(2,1)}), bf16[128,32,512]{2,1,0:T(8,128)(2,1)}, u32[]{:S(2)}, u32[]{:S(2)}) async-start(bf16[128,32,512]{2,1,0:T(8,128)(2,1)} %copy.14), calls=%async_computation | async-start | bytes 8388608 | tf_op jit(solution)/shard_map/all_to_all | solution.py:153
  23.3 0.0 copy-done.2
  23.3 0.1 copy.37
  23.4 1.4 collective-permute-start.3
  24.8 13.4 %collective-permute-done.3 = f32[2,32,512]{2,1,0:T(8,128)S(1)} collective-permute-done((f32[2,32,512]{2,1,0:T(8,128)S(1)}, f32[2,32,512]{2,1,0:T(8,128)S(1)}, u32[]{:S(2)}, u32[]{:S(2)}) %collective-permute-start.3) | collective-permute-done | bytes 131104 | tf_op jit(solution)/shard_map/ppermute | solution.py:121
  38.3 82.3 %all-to-all-done = bf16[128,32,512]{2,1,0:T(8,128)(2,1)} async-done(((bf16[128,32,512]{2,1,0:T(8,128)(2,1)}), bf16[128,32,512]{2,1,0:T(8,128)(2,1)}, u32[]{:S(2)}, u32[]{:S(2)}) %all-to-all-start) | async-done | bytes 4194336 | tf_op jit(solution)/shard_map/all_to_all | solution.py:153
  120.6 0.0 copy-done
  120.6 3.7 %fusion.24 = s16[4,64,512]{2,1,0:T(8,128)(2,1)S(1)} fusion(bf16[4096,512,1]{1,0,2:T(8,128)(2,1)} %bitcast.5, bf16[64,4,4096]{2,1,0:T(4,128)(2,1)S(1)} %copy-done), kind=kOutput, calls=%fused_computation.13 | convolution fusion | flops 1074921472 | bytes 6553600 | tf_op jit(solution)/shard_map/akm,mz->kaz/dot_general | solution.py:159
  124.4 1.4 collective-permute-start
  125.9 0.1 collective-permute-start.4
  126.0 2.0 %collective-permute-start.5 = (f32[2,8,1024]{2,1,0:T(8,128)S(1)}, f32[2,8,1024]{2,1,0:T(8,128)S(1)}, u32[]{:S(2)}, u32[]{:S(2)}) collective-permute-start(f32[2,8,1024]{2,1,0:T(8,128)S(1)} %get-tuple-element.9), channel_id=1, source_target_pairs={{0,255},{1,0},{2,1},{3,2},{4,3},{5,4},{6,5},{7,6},{8,7},{9,8},{10,... | collective-permute-start | bytes 196616 | tf_op jit(solution)/shard_map/ppermute | solution.py:125
  128.0 1.9 %collective-permute-done = s16[4,32,512]{2,1,0:T(8,128)(2,1)S(1)} collective-permute-done((s16[4,32,512]{2,1,0:T(8,128)(2,1)S(1)}, s16[4,32,512]{2,1,0:T(8,128)(2,1)S(1)}, u32[]{:S(2)}, u32[]{:S(2)}) %collective-permute-start) | collective-permute-done | bytes 131104 | tf_op jit(solution)/shard_map/ppermute | solution.py:121
  129.9 0.1 add_select_fusion.1
  130.0 4.0 %collective-permute-start.2 = (s16[4,8,1024]{2,1,0:T(8,128)(2,1)S(1)}, s16[4,8,1024]{2,1,0:T(8,128)(2,1)S(1)}, u32[]{:S(2)}, u32[]{:S(2)}) collective-permute-start(s16[4,8,1024]{2,1,0:T(8,128)(2,1)S(1)} %get-tuple-element.13), channel_id=1, source_target_pairs={{0,255},{1,0},{2,1},{3,2},{4,3},{5,4},{6,5},{7,6},{8,7},{9,8},{10,... | collective-permute-start | bytes 196616 | tf_op jit(solution)/shard_map/ppermute | solution.py:125
  134.0 0.0 collective-permute-start.1
  134.0 0.1 add_select_fusion.code
  134.1 0.0 collective-permute-done.4.field_left
  134.1 0.0 collective-permute-done.5.field_right
  134.1 1.8 %collective-permute-done.2 = s16[4,8,1024]{2,1,0:T(8,128)(2,1)S(1)} collective-permute-done((s16[4,8,1024]{2,1,0:T(8,128)(2,1)S(1)}, s16[4,8,1024]{2,1,0:T(8,128)(2,1)S(1)}, u32[]{:S(2)}, u32[]{:S(2)}) %collective-permute-start.2) | collective-permute-done | bytes 65568 | tf_op jit(solution)/shard_map/ppermute | solution.py:125
  135.9 2.4 %collective-permute-done.1 = s16[4,8,1024]{2,1,0:T(8,128)(2,1)S(1)} collective-permute-done((s16[4,8,1024]{2,1,0:T(8,128)(2,1)S(1)}, s16[4,8,1024]{2,1,0:T(8,128)(2,1)S(1)}, u32[]{:S(2)}, u32[]{:S(2)}) %collective-permute-start.1) | collective-permute-done | bytes 65568 | tf_op jit(solution)/shard_map/ppermute | solution.py:125
  138.3 0.0 copy-start.1
  138.3 3.4 %copy-done.1 = bf16[2,2,1024,1024]{3,2,1,0:T(8,128)(2,1)S(1)} copy-done((bf16[2,2,1024,1024]{3,2,1,0:T(8,128)(2,1)S(1)}, bf16[2,2,1024,1024]{3,2,1,0:T(8,128)(2,1)}, u32[]{:S(2)}) %copy-start.1) | copy-done | bytes 8388632
  141.7 7.4 %march.1 = (f32[2,32,512]{2,1,0:T(8,128)S(1)}, bf16[2,32,512]{2,1,0:T(8,128)(2,1)S(1)}) custom-call(s32[1]{0:T(128)} %bitcast.side, s16[128,1024]{1,0:T(8,128)(2,1)S(1)} %add_select_fusion.code, s16[32,1024]{1,0:T(8,128)(2,1)S(1)} %bitcast.35, s16[32,1024]{1,0:T(8,128)(2,1)S(1)} %bitcast.34, f32[2,32,1024]{2,1,0:T(8,128)S(1)} %maximum_select_fusion.field, ...), custom_call_target="tpu_custom_call" | custom-call | flops 3221225472 | bytes 10485760 | tf_op jit(solution)/shard_map/march/pallas_call | solution.py:102
  149.0 5.2 %collective-permute-start.6 = (bf16[2,32,512]{2,1,0:T(8,128)(2,1)S(1)}, bf16[2,32,512]{2,1,0:T(8,128)(2,1)S(1)}, u32[]{:S(2)}, u32[]{:S(2)}) collective-permute-start(bf16[2,32,512]{2,1,0:T(8,128)(2,1)S(1)} %get-tuple-element.8), channel_id=1, source_target_pairs={{0,1},{1,0},{2,3},{3,2},{4,5},{5,4},{6,7},{7,6},{8,9},{9,8},{10,11... | collective-permute-start | bytes 196616 | tf_op jit(solution)/shard_map/ppermute | solution.py:121
  154.3 2.2 %collective-permute-done.6 = bf16[2,32,512]{2,1,0:T(8,128)(2,1)S(1)} collective-permute-done((bf16[2,32,512]{2,1,0:T(8,128)(2,1)S(1)}, bf16[2,32,512]{2,1,0:T(8,128)(2,1)S(1)}, u32[]{:S(2)}, u32[]{:S(2)}) %collective-permute-start.6) | collective-permute-done | bytes 65568 | tf_op jit(solution)/shard_map/ppermute | solution.py:121
  156.5 0.9 copy.17
  (7 shorter events, 0.1 us)
Async XLA Ops:
  0.0 120.6 %copy-start = (bf16[64,4,4096]{2,1,0:T(4,128)(2,1)S(1)}, bf16[64,4,4096]{2,1,0:T(4,128)(2,1)}, u32[]{:S(2)}) copy-start(bf16[64,4,4096]{2,1,0:T(4,128)(2,1)} %param.10) | copy-start | bytes 6291460
  7.7 15.6 %copy-start.2 = (f32[64,2,512]{2,1,0:T(2,128)S(1)}, f32[64,2,512]{2,1,0:T(2,128)}, u32[]{:S(2)}) copy-start(f32[64,2,512]{2,1,0:T(2,128)} %param.6) | copy-start | bytes 786436
  7.7 112.9 %all-to-all-start = ((bf16[128,32,512]{2,1,0:T(8,128)(2,1)}), bf16[128,32,512]{2,1,0:T(8,128)(2,1)}, u32[]{:S(2)}, u32[]{:S(2)}) async-start(bf16[128,32,512]{2,1,0:T(8,128)(2,1)} %copy.14), calls=%async_computation | async-start | bytes 8388608 | tf_op jit(solution)/shard_map/all_to_all | solution.py:153
  23.4 14.9 %collective-permute-start.3 = (f32[2,32,512]{2,1,0:T(8,128)S(1)}, f32[2,32,512]{2,1,0:T(8,128)S(1)}, u32[]{:S(2)}, u32[]{:S(2)}) collective-permute-start(f32[2,32,512]{2,1,0:T(8,128)S(1)} %get-tuple-element.12), channel_id=1, source_target_pairs={{0,1},{1,0},{2,3},{3,2},{4,5},{5,4},{6,7},{7,6},{8,9},{9,8},{10,11... | collective-permute-start | bytes 393224 | tf_op jit(solution)/shard_map/ppermute | solution.py:121
  124.4 5.5 %collective-permute-start = (s16[4,32,512]{2,1,0:T(8,128)(2,1)S(1)}, s16[4,32,512]{2,1,0:T(8,128)(2,1)S(1)}, u32[]{:S(2)}, u32[]{:S(2)}) collective-permute-start(s16[4,32,512]{2,1,0:T(8,128)(2,1)S(1)} %get-tuple-element.16), channel_id=1, source_target_pairs={{0,1},{1,0},{2,3},{3,2},{4,5},{5,4},{6,7},{7,6},{8,9},{9,8},{10,11... | collective-permute-start | bytes 393224 | tf_op jit(solution)/shard_map/ppermute | solution.py:121
  125.9 8.2 %collective-permute-start.4 = (f32[2,8,1024]{2,1,0:T(8,128)S(1)}, f32[2,8,1024]{2,1,0:T(8,128)S(1)}, u32[]{:S(2)}, u32[]{:S(2)}) collective-permute-start(f32[2,8,1024]{2,1,0:T(8,128)S(1)} %get-tuple-element.10), channel_id=1, source_target_pairs={{0,1},{1,2},{2,3},{3,4},{4,5},{5,6},{6,7},{7,8},{8,9},{9,10},{10,1... | collective-permute-start | bytes 196616 | tf_op jit(solution)/shard_map/ppermute | solution.py:125
  126.0 8.2 %collective-permute-start.5 = (f32[2,8,1024]{2,1,0:T(8,128)S(1)}, f32[2,8,1024]{2,1,0:T(8,128)S(1)}, u32[]{:S(2)}, u32[]{:S(2)}) collective-permute-start(f32[2,8,1024]{2,1,0:T(8,128)S(1)} %get-tuple-element.9), channel_id=1, source_target_pairs={{0,255},{1,0},{2,1},{3,2},{4,3},{5,4},{6,5},{7,6},{8,7},{9,8},{10,... | collective-permute-start | bytes 196616 | tf_op jit(solution)/shard_map/ppermute | solution.py:125
  130.0 5.9 %collective-permute-start.2 = (s16[4,8,1024]{2,1,0:T(8,128)(2,1)S(1)}, s16[4,8,1024]{2,1,0:T(8,128)(2,1)S(1)}, u32[]{:S(2)}, u32[]{:S(2)}) collective-permute-start(s16[4,8,1024]{2,1,0:T(8,128)(2,1)S(1)} %get-tuple-element.13), channel_id=1, source_target_pairs={{0,255},{1,0},{2,1},{3,2},{4,3},{5,4},{6,5},{7,6},{8,7},{9,8},{10,... | collective-permute-start | bytes 196616 | tf_op jit(solution)/shard_map/ppermute | solution.py:125
  134.0 4.3 %collective-permute-start.1 = (s16[4,8,1024]{2,1,0:T(8,128)(2,1)S(1)}, s16[4,8,1024]{2,1,0:T(8,128)(2,1)S(1)}, u32[]{:S(2)}, u32[]{:S(2)}) collective-permute-start(s16[4,8,1024]{2,1,0:T(8,128)(2,1)S(1)} %get-tuple-element.14), channel_id=1, source_target_pairs={{0,1},{1,2},{2,3},{3,4},{4,5},{5,6},{6,7},{7,8},{8,9},{9,10},{10,1... | collective-permute-start | bytes 196616 | tf_op jit(solution)/shard_map/ppermute | solution.py:125
  138.3 3.4 %copy-start.1 = (bf16[2,2,1024,1024]{3,2,1,0:T(8,128)(2,1)S(1)}, bf16[2,2,1024,1024]{3,2,1,0:T(8,128)(2,1)}, u32[]{:S(2)}) copy-start(bf16[2,2,1024,1024]{3,2,1,0:T(8,128)(2,1)} %factors.1) | copy-start | bytes 25165828
  149.0 7.5 %collective-permute-start.6 = (bf16[2,32,512]{2,1,0:T(8,128)(2,1)S(1)}, bf16[2,32,512]{2,1,0:T(8,128)(2,1)S(1)}, u32[]{:S(2)}, u32[]{:S(2)}) collective-permute-start(bf16[2,32,512]{2,1,0:T(8,128)(2,1)S(1)} %get-tuple-element.8), channel_id=1, source_target_pairs={{0,1},{1,0},{2,3},{3,2},{4,5},{5,4},{6,7},{7,6},{8,9},{9,8},{10,11... | collective-permute-start | bytes 196616 | tf_op jit(solution)/shard_map/ppermute | solution.py:121
